TPU v7x, 256 devices: a whole 4x4x8 slice. The times are simulated.
256 devices in a mesh: row: 32 (over z, x_hi, core), col: 8 (over x_lo, y).
Axes of the slice: x: 4 (x_hi: 2, x_lo: 2; x = x_hi * 2 + x_lo), y: 4, z: 8, core: 2. Of those that a mesh axis runs over, the one named last changes fastest.
Arguments:
- queries: bfloat16 [16384, 4096], P(('row', 'col')), may hold values from -160 to 160
- keys: bfloat16 [16384, 512], P(('col', 'row')), may hold values from -6 to 6
- values: bfloat16 [16384, 512], P(('col', 'row')), may hold values from -6 to 6
- doc_lengths: int32 [16], replicated, may hold values from 1 to 8192, 16384 in all
Outputs:
- attended: bfloat16 [16384, 4096], P(('row', 'col'))
Inputs may be any that keep to these rules, and one draw needn't show every extreme that they name: `doc_lengths`: the lengths sum to 16384; one document has exactly 8192 tokens.
All inputs are finite; a program needn't handle non-finite values.
Results may differ from a plain program's by a relative error of at most 0.015.
Values may be sent and summed in bfloat16 or wider, within the bound.
A program may use at most 256 MiB of HBM per device.

v0:
```python
import jax
import jax.numpy as jnp
from jax import lax
from jax.sharding import PartitionSpec as P

QUERY_HEADS = 32
KEY_VALUE_HEADS = 4
HEAD_SIZE = 128
QUERY_PER_KEY = 8


def doc_of(positions, doc_ends):
    return jnp.sum((positions[:, None] >= doc_ends[None, :]).astype(jnp.int32), axis=1)


def body(queries, keys, values, doc_lengths):
    rows_own = queries.shape[0]
    n_row = lax.axis_size("row")
    row_index = lax.axis_index("row")
    col_index = lax.axis_index("col")
    gathered_rows = lax.all_gather(queries, "col", axis=0, tiled=True)
    query_count = gathered_rows.shape[0]
    grouped_rows = query_count * QUERY_PER_KEY
    head_major = (
        gathered_rows.reshape(query_count, KEY_VALUE_HEADS, QUERY_PER_KEY, HEAD_SIZE)
        .transpose(1, 0, 2, 3)
        .reshape(KEY_VALUE_HEADS, grouped_rows, HEAD_SIZE)
    )
    doc_ends = jnp.cumsum(doc_lengths)
    query_pos = row_index * query_count + jnp.arange(query_count, dtype=jnp.int32)
    query_doc = doc_of(query_pos, doc_ends)
    key_base = col_index * (n_row * rows_own)
    scale = 1.0 / HEAD_SIZE**0.5

    def visibility(key_start, window_width):
        key_pos = key_base + key_start + jnp.arange(window_width, dtype=jnp.int32)
        key_doc = doc_of(key_pos, doc_ends)
        return (key_pos[None, :] <= query_pos[:, None]) & (key_doc[None, :] == query_doc[:, None])

    def tile_step(state, key_tile, value_tile, key_start):
        old_max, old_total, old_sums = state
        window_width = key_tile.shape[0]
        visible = visibility(key_start, window_width)
        mask_rows = jnp.broadcast_to(
            visible[:, None, :], (query_count, QUERY_PER_KEY, window_width)
        ).reshape(1, grouped_rows, window_width)
        scores = (
            jnp.einsum("hrd,khd->hrk", head_major, key_tile, preferred_element_type=jnp.float32)
            * scale
        )
        new_max = jnp.maximum(old_max, jnp.max(jnp.where(mask_rows, scores, -1e30), axis=2))
        weights = jnp.where(mask_rows, jnp.exp(scores - new_max[..., None]), 0.0)
        factor = jnp.exp(old_max - new_max)
        new_total = old_total * factor + jnp.sum(weights, axis=2)
        product = jnp.einsum(
            "hrk,khd->hrd",
            weights.astype(jnp.bfloat16),
            value_tile,
            preferred_element_type=jnp.float32,
        )
        return (new_max, new_total, old_sums * factor[..., None] + product)

    initial = (
        jnp.full((KEY_VALUE_HEADS, grouped_rows), -1e30, jnp.float32),
        jnp.zeros((KEY_VALUE_HEADS, grouped_rows), jnp.float32),
        jnp.zeros((KEY_VALUE_HEADS, grouped_rows, HEAD_SIZE), jnp.float32),
    )
    key_rows = lax.all_gather(keys, "row", axis=0, tiled=True)
    value_rows = lax.all_gather(values, "row", axis=0, tiled=True)
    window_width = key_rows.shape[0]
    rows_per_step = 1
    for option in range(1, 129):
        if window_width % option == 0:
            rows_per_step = option
    steps_count = window_width // rows_per_step
    key_window = key_rows.reshape(steps_count, rows_per_step, KEY_VALUE_HEADS, HEAD_SIZE)
    value_window = value_rows.reshape(steps_count, rows_per_step, KEY_VALUE_HEADS, HEAD_SIZE)
    offsets = rows_per_step * jnp.arange(steps_count, dtype=jnp.int32)

    def scan_step(state, inputs):
        key_tile, value_tile, offset = inputs
        return (tile_step(state, key_tile, value_tile, offset), None)

    def run_all(state):
        result, unused = lax.scan(scan_step, state, (key_window, value_window, offsets))
        return result

    last_pos = key_base + window_width - 1
    first_doc = doc_of(jnp.reshape(key_base, (1,)), doc_ends)[0]
    last_doc = doc_of(jnp.reshape(last_pos, (1,)), doc_ends)[0]
    seen = (
        (key_base <= query_pos[query_count - 1])
        & (last_doc >= query_doc[0])
        & (first_doc <= query_doc[query_count - 1])
    )
    head_best, head_total, head_sums = lax.cond(seen, run_all, lambda state: state, initial)
    row_best = head_best.reshape(KEY_VALUE_HEADS, query_count, QUERY_PER_KEY).transpose(1, 0, 2)
    row_total = head_total.reshape(KEY_VALUE_HEADS, query_count, QUERY_PER_KEY).transpose(1, 0, 2)
    row_sums = head_sums.reshape(KEY_VALUE_HEADS, query_count, QUERY_PER_KEY, HEAD_SIZE).transpose(
        1, 0, 2, 3
    )
    top = lax.pmax(row_best.astype(jnp.bfloat16), "col").astype(row_best.dtype)
    factor = jnp.exp(row_best - top)
    own_sums, own_total = (
        lax.psum_scatter(
            (row_sums * factor[..., None]).astype(jnp.bfloat16),
            "col",
            scatter_dimension=0,
            tiled=True,
        ).astype(jnp.float32),
        lax.psum_scatter(
            (row_total * factor).astype(jnp.bfloat16), "col", scatter_dimension=0, tiled=True
        ).astype(jnp.float32),
    )
    output = own_sums / own_total[..., None]
    return output.reshape(rows_own, QUERY_HEADS * HEAD_SIZE).astype(jnp.bfloat16)


def solution(mesh):
    return jax.shard_map(
        body,
        mesh=mesh,
        in_specs=(P(("row", "col"), None), P(("col", "row"), None), P(("col", "row"), None), P()),
        out_specs=P(("row", "col"), None),
        check_vma=False,
    )
```

profile of v0, /device:TPU:8, one launch (start us, length us, event | category | flops | bytes accessed | tf_op | source)
XLA Modules:
  0.0 728.3 jit_solution(5163540946129905244)
XLA Ops:
  6.5 0.7 all-gather.8.cloned.1.call-update
  7.3 0.7 all-gather.4.cloned.1.call-update
  8.1 0.7 all-gather.6.cloned.1.call-update
  10.0 0.7 copy.64
  10.8 0.7 convert_reduce_fusion.2
  11.6 0.6 fusion.20
  14.6 50.4 %all-gather.8.cloned.1.call-done = bf16[512,4096]{1,0:T(8,128)(2,1)} async-done(((bf16[64,4096]{1,0:T(8,128)(2,1)}), bf16[512,4096]{1,0:T(8,128)(2,1)}) %all-gather.8.cloned.1.call-update) | async-done | bytes 4194320 | tf_op jit(solution)/shard_map/all_gather | solution.py:21
  65.0 6.5 copy.65
  71.5 77.2 %all-gather.4.cloned.1.call-done = bf16[2048,512]{1,0:T(8,128)(2,1)} async-done(((bf16[64,512]{1,0:T(8,128)(2,1)}), bf16[2048,512]{1,0:T(8,128)(2,1)}) %all-gather.4.cloned.1.call-update) | async-done | bytes 2097168 | tf_op jit(solution)/shard_map/all_gather | solution.py:68
  148.8 79.4 %all-gather.6.cloned.1.call-done = bf16[2048,512]{1,0:T(8,128)(2,1)} async-done(((bf16[64,512]{1,0:T(8,128)(2,1)}), bf16[2048,512]{1,0:T(8,128)(2,1)}) %all-gather.6.cloned.1.call-update) | async-done | bytes 2097168 | tf_op jit(solution)/shard_map/all_gather | solution.py:69
  228.2 5.0 conditional.1
  228.2 0.6 broadcast_in_dim.25
  228.8 0.6 broadcast_in_dim.26
  229.4 3.8 broadcast_in_dim.31
  233.2 1.4 reshape.152
  234.9 388.4 %pmax.7 = bf16[512,4,8]{0,2,1:T(8,128)(2,1)S(1)} all-reduce(bf16[512,4,8]{0,2,1:T(8,128)(2,1)S(1)} %bitcast_convert_fusion), channel_id=1, replica_groups=mesh['row'=32,'col'=8] {'col'}, use_global_device_ids=true, to_apply=%region_11.12 | all-reduce | flops 16384 | bytes 65536 | tf_op jit(solution)/shard_map/pmax | solution.py:102
  623.4 1.4 reshape.153
  625.2 0.8 copy.81
  626.4 6.8 fusion.15
  633.3 28.4 %reduce-scatter.7.cloned.1.call-done = bf16[64,32]{1,0:T(8,128)(2,1)} async-done(((bf16[512,32]{1,0:T(8,128)(2,1)}), bf16[64,32]{1,0:T(8,128)(2,1)}) %reduce-scatter.7.cloned.1.call-update) | async-done | bytes 4112
  661.7 0.8 copy.82
  662.6 56.7 %reduce-scatter.5.cloned.1.call-done = bf16[64,4,8,128]{3,2,1,0:T(8,128)(2,1)} async-done(((bf16[512,4,8,128]{3,2,1,0:T(8,128)(2,1)}), bf16[64,4,8,128]{3,2,1,0:T(8,128)(2,1)}) %reduce-scatter.5.cloned.1.call-update) | async-done | bytes 524304 | tf_op jit(solution)/shard_map/reduce_scatter | solution.py:105
  719.3 1.4 divide_convert_fusion
  720.7 1.0 copy.94
  (19 shorter events, 2.1 us)
Async XLA Ops:
  6.5 58.5 %all-gather.8.cloned.1.call-start = ((), (), s32[]{:S(2)}) async-start(), calls=%async_computation.4 | async-start | bytes 4718592 | tf_op jit(solution)/shard_map/all_gather | solution.py:21
  7.3 141.5 %all-gather.4.cloned.1.call-start = ((), (), s32[]{:S(2)}) async-start(), calls=%async_computation.2 | async-start | bytes 2162688 | tf_op jit(solution)/shard_map/all_gather | solution.py:68
  8.0 220.2 %all-gather.6.cloned.1.call-start = ((), (), s32[]{:S(2)}) async-start(), calls=%async_computation.3 | async-start | bytes 2162688 | tf_op jit(solution)/shard_map/all_gather | solution.py:69
  8.7 652.9 %reduce-scatter.7.cloned.1.call-start = ((), (), s32[]{:S(2)}) async-start(), calls=%async_computation.6 | async-start | bytes 147456
  625.9 93.4 %reduce-scatter.5.cloned.1.call-start = ((), (), s32[]{:S(2)}) async-start(), calls=%async_computation.5 | async-start | bytes 4718592 | tf_op jit(solution)/shard_map/reduce_scatter | solution.py:105
Sparse Core Ops, SparseCore 0:
  9.1 55.8 all-gather.7
  67.8 80.9 all-gather.3
  151.6 76.5 all-gather.5
  626.1 35.5 reduce-scatter.6
  664.2 55.0 reduce-scatter.4
where the time goes:
time: 735 us; the launch traced here: 728 us
  blocking collectives  388 us (53%)
  waiting for transfers between devices  294 us (40%)
  local copies, waits for them, and re-layouts  20 us (3%)
  between operations  16.3 us (2%)
  other arithmetic  9.1 us (1%)
    pmax x1, blocking collectives, body(): top = lax.pmax(row_best.astype(jnp.bfloat16), 'col').astype(row_best.dtype)  388 us
    all_gather x1, waiting for transfers between devices, body(): value_rows = lax.all_gather(values, 'row', axis=0, tiled=True)  79.4 us
    all_gather x1, waiting for transfers between devices, body(): key_rows = lax.all_gather(keys, 'row', axis=0, tiled=True)  77.2 us
    reduce_scatter x1, waiting for transfers between devices, body(): lax.psum_scatter((row_sums * factor[..., None]).astype(jnp.bfloat16), 'co...  56.7 us
    all_gather x1, waiting for transfers between devices, body(): gathered_rows = lax.all_gather(queries, 'col', axis=0, tiled=True)  50.4 us
    unnamed x6, waiting for transfers between devices  30.5 us
  transfers between devices with their start and end apart: 5, of which 5 were waited for; matrix products, arithmetic and copies ran while one was open for 2% of the time, Pallas kernels for 0%

commit v1 on v0

v1 whole, which is shorter than its diff:
```python
import jax
import jax.numpy as jnp
from jax import lax
from jax.experimental import pallas as pl
from jax.experimental.pallas import tpu as pltpu
from jax.sharding import PartitionSpec as P

D = 128
G = 8
BF = jnp.bfloat16
F32 = jnp.float32
LOG2E = 1.4426950408889634
SCALE = LOG2E / D**0.5
HIDE = -1e30
FLOOR = -3e30
PIECE = 256
ROWS = 512
VR = 144
MESH = pl.DeviceIdType.MESH


def kernel(
    lengths,
    queries,
    keys,
    values,
    out,
    q_in,
    sub,
    kv,
    q_aug,
    kd,
    vt,
    acc,
    top,
    sb,
    mb,
    o_send,
    y_send,
    y_recv,
    x_send,
    x_recv,
    c_send,
    c_recv,
    o_ssem,
    o_rsem,
    l_sem,
):
    row = lax.axis_index("row")
    col = lax.axis_index("col")
    z = row // 4
    x_hi = (row // 2) % 2
    core = row % 2
    x_lo = col // 4
    y = col % 4
    x = x_hi * 2 + x_lo
    rank = x_hi * 4 + core * 2 + x_lo
    first = z * 2048 + rank * 256
    up = (lax.rem(row + 4, 32), col)
    down = (lax.rem(row + 28, 32), col)
    twin = (row + 1 - 2 * core, col)

    def at_y(d):
        return (row, x_lo * 4 + lax.rem(y + d, 4))

    def at_x(d, k):
        xd = lax.rem(x + d, 4)
        return (z * 4 + (xd // 2) * 2 + k, (xd % 2) * 4 + y)

    barrier = pltpu.get_barrier_semaphore()
    for d in (1, 2, 3):
        pl.semaphore_signal(barrier, inc=1, device_id=at_y(d), device_id_type=MESH)
    for d in (1, 2, 3):
        for k in (0, 1):
            pl.semaphore_signal(barrier, inc=1, device_id=at_x(d, k), device_id_type=MESH)
    for who in (twin, up, down):
        pl.semaphore_signal(barrier, inc=1, device_id=who, device_id_type=MESH)

    def cut(ref, head, width):
        return ref.at[:, pl.ds(pl.multiple_of(head * width, width), width)]

    def own_copies():
        return (
            pltpu.make_async_copy(cut(keys, y, D), sub.at[y, :, 0:D], l_sem.at[0]),
            pltpu.make_async_copy(cut(values, y, D), sub.at[y, :, D : 2 * D], l_sem.at[1]),
            pltpu.make_async_copy(cut(queries, y, G * D), q_in.at[y], l_sem.at[2]),
        )

    def y_copy(kind, d):
        head = lax.rem(y + d, 4)
        src, dst = (
            (cut(keys, head, D), sub.at[y, :, 0:D]),
            (cut(values, head, D), sub.at[y, :, D : 2 * D]),
            (cut(queries, head, G * D), q_in.at[y]),
        )[kind]
        return pltpu.make_async_remote_copy(
            src_ref=src,
            dst_ref=dst,
            send_sem=y_send.at[kind, d - 1],
            recv_sem=y_recv.at[kind, d - 1],
            device_id=at_y(d),
            device_id_type=MESH,
        )

    def y_wait(kind, d):
        peer = lax.rem(y + 4 - d, 4)
        dst = (sub.at[peer, :, 0:D], sub.at[peer, :, D : 2 * D], q_in.at[peer])[kind]
        pltpu.make_async_remote_copy(
            src_ref=dst,
            dst_ref=dst,
            send_sem=y_send.at[kind, d - 1],
            recv_sem=y_recv.at[kind, d - 1],
            device_id=at_y(d),
            device_id_type=MESH,
        ).wait_recv()

    for copy in own_copies():
        copy.start()

    acc[...] = jnp.zeros_like(acc)
    top[...] = jnp.full_like(top, FLOOR)
    vt[:, D:VR, :] = jnp.ones((2, VR - D, 4 * PIECE), BF)

    lane = lax.broadcasted_iota(jnp.int32, (1, D), 1)
    doc_first = jnp.zeros((1, D), jnp.int32)
    doc_end = jnp.zeros((1, D), jnp.int32)
    total = jnp.int32(0)
    for d in range(16):
        doc_first = jnp.where(lane == d, total, doc_first)
        total = total + lengths[d]
        doc_end = jnp.where(lane == d, total, doc_end)

    def in_doc(start, count):
        pos = start + lax.broadcasted_iota(jnp.int32, (count, D), 0)
        return (pos >= doc_first) & (pos < doc_end)

    pl.semaphore_wait(barrier, 12)
    for kind in (0, 1, 2):
        for d in (1, 3, 2):
            y_copy(kind, d).start()
    own = own_copies()
    own[0].wait()
    own[1].wait()
    for d in (1, 3, 2):
        y_wait(0, d)
        y_wait(1, d)

    def x_slot(chunk, who):
        rows = pl.ds(pl.multiple_of(who * 64, 64), 64)
        return kv.at[chunk * 8 + z, rows, :]

    def x_copy(d, j):
        chunk = x_lo * 4 + j
        return pltpu.make_async_remote_copy(
            src_ref=sub.at[j],
            dst_ref=x_slot(chunk, x_hi * 2 + core),
            send_sem=x_send.at[d, j],
            recv_sem=x_recv.at[chunk, x_hi * 2 + core],
            device_id=at_x(d, j % 2),
            device_id_type=MESH,
        )

    def x_local(j):
        chunk = x_lo * 4 + j
        return pltpu.make_async_copy(
            sub.at[j],
            x_slot(chunk, x_hi * 2 + core),
            x_recv.at[chunk, x_hi * 2 + core],
        )

    for j in range(4):

        @pl.when(core == j % 2)
        def _():
            x_local(j).start()

        @pl.when(core != j % 2)
        def _():
            x_copy(0, j).start()

        for d in (1, 3, 2):
            x_copy(d, j).start()

    own[2].wait()
    for d in (1, 3, 2):
        y_wait(2, d)

    for b in range(4):
        seen = in_doc(first + b * 64, 64)
        lanes = lax.broadcasted_iota(jnp.int32, (64, D), 1)
        wall = jnp.where(lanes < 16, jnp.where(seen, 0.0, HIDE), jnp.where(lanes == 16, HIDE, 0.0))
        wall = wall.astype(BF)
        for h in range(G):
            at = (b * G + h) * 64
            q_aug[at : at + 64, 0:D] = q_in[b, :, h * D : (h + 1) * D]
            q_aug[at : at + 64, D : 2 * D] = wall

    def route(chunk):
        last = jnp.minimum(chunk + 4, 7)
        before = jnp.where(chunk < 4, 1, 2)
        behind = jnp.maximum(chunk, 3) - before
        most_up = before + last - chunk
        most_down = behind + last - chunk
        u = lax.rem(z - chunk + before + 16, 8)
        v = lax.rem(last + behind - z + 16, 8)
        in_up = u <= most_up
        in_down = v <= most_down
        got_up = jnp.where(in_up, u, 0)
        got_down = jnp.where(in_down, v, 0)
        on_up = in_up & (u < most_up)
        on_down = in_down & (v < most_down)
        wanted = (z >= chunk) & (z <= chunk + 4)
        return got_up, got_down, on_up, on_down, wanted

    def source(got_up, got_down, i):
        both = jnp.minimum(got_up, got_down)
        paired = i <= 2 * both
        step = jnp.where(paired, (i + 1) // 2, i - both)
        rising = jnp.where(paired, lax.rem(i, 2) == 1, got_up > got_down)
        return lax.rem(jnp.where(rising, z - step, z + step) + 8, 8), rising

    def c_copy(way, piece):
        return pltpu.make_async_remote_copy(
            src_ref=kv.at[piece],
            dst_ref=kv.at[piece],
            send_sem=c_send.at[way, piece],
            recv_sem=c_recv.at[piece],
            device_id=(up, down, twin)[way],
            device_id_type=MESH,
        )

    def serve(i, act):
        def one(chunk, carry):
            got_up, got_down, on_up, on_down, wanted = route(chunk)
            src, rising = source(got_up, got_down, i)
            src = jnp.where(i == 0, z, src)
            piece = chunk * 8 + src
            mine = lax.rem(chunk, 2) == core
            there = i <= got_up + got_down
            go_up = mine & there & on_up & ((i == 0) | rising)
            go_down = mine & there & on_down & ((i == 0) | jnp.logical_not(rising))
            go_twin = mine & there & wanted
            if act:

                @pl.when(mine & (i == 0))
                def _():
                    for who in range(4):
                        pltpu.make_async_copy(
                            sub.at[0], x_slot(chunk, who), x_recv.at[chunk, who]
                        ).wait()

                @pl.when(there & ((mine & (i > 0)) | (jnp.logical_not(mine) & wanted)))
                def _():
                    c_copy(0, piece).wait_recv()

            for way, go in ((0, go_up), (1, go_down), (2, go_twin)):

                @pl.when(go)
                def _():
                    if act:
                        c_copy(way, piece).start()
                    else:
                        c_copy(way, piece).wait_send()

            return carry

        lax.fori_loop(0, 8, one, 0)

    def w_piece(step):
        src = lax.rem(z + step + 8, 8)
        chunk = jnp.where(src < rank, z, z - 4)
        live = chunk >= 0
        return jnp.where(live, chunk, z), jnp.where(live, src, z), live

    def pieces(i):
        got = []
        for back in (3, 2, 1):
            chunk = z - back
            live = chunk >= 0
            got_up, got_down, _, _, _ = route(jnp.maximum(chunk, 0))
            src, _ = source(got_up, got_down, i)
            src = jnp.where(i == 0, z, src)
            got.append((jnp.where(live, chunk, z), jnp.where(live, src, z), live))
        step = jnp.where(i == 1, -1, 0)
        step = jnp.where(i == 2, 1, step)
        step = jnp.where(i == 4, 2, step)
        step = jnp.where(i == 6, 4, step)
        step = jnp.where(i == 7, -3, step)
        chunk, src, live = w_piece(step)
        got.append((chunk, src, live & (i != 3) & (i != 5)))
        return got

    def ready(half, got):
        for n, (chunk, src, live) in enumerate(got):
            piece = chunk * 8 + src
            at = slice(n * PIECE, (n + 1) * PIECE)
            vt[half, 0:D, at] = kv[piece, :, D : 2 * D].T
            seen = in_doc(chunk * 2048 + src * 256, PIECE)
            lanes = lax.broadcasted_iota(jnp.int32, (PIECE, D), 1)
            flag = jnp.where(live, jnp.where(seen, 1.0, 0.0), jnp.where(lanes == 16, 1.0, 0.0))
            kd[at, :] = flag.astype(BF)

    def block(r):
        return pl.ds(pl.multiple_of(r * ROWS, ROWS), ROWS)

    def score(got, r, slot, diagonal=False):
        q = q_aug[block(r), :]
        best = None
        for n, (chunk, src, _) in enumerate(got):
            at = slice(n * PIECE, (n + 1) * PIECE)
            k = jnp.concatenate([kv[chunk * 8 + src, :, 0:D], kd[at, :]], axis=1)
            s = lax.dot_general(k, q, (((1,), (1,)), ((), ())), preferred_element_type=F32)
            if diagonal and n == len(got) - 1:
                key = lax.broadcasted_iota(jnp.int32, (PIECE, ROWS), 0)
                query = r * 64 + (lax.broadcasted_iota(jnp.int32, (PIECE, ROWS), 1) & 63)
                s = jnp.where(key <= query, s, HIDE)
            sb[slot, at, :] = s
            here = jnp.max(s, axis=0, keepdims=True)
            best = here if best is None else jnp.maximum(best, here)
        mb[slot, 0:1, :] = best

    def mix(half, count, r, slot):
        cols = block(r)
        old = top[0:1, cols]
        new = jnp.maximum(old, mb[slot, 0:1, :])
        shift = new * SCALE
        sums = acc[:, cols] * jnp.exp2((old - new) * SCALE)
        for n in range(count):
            at = slice(n * PIECE, (n + 1) * PIECE)
            w = jnp.exp2(sb[slot, at, :] * SCALE - shift).astype(BF)
            sums = sums + jnp.dot(vt[half, :, at], w, preferred_element_type=F32)
        acc[:, cols] = sums
        top[0:1, cols] = new

    serve(jnp.int32(0), True)
    start = pieces(jnp.int32(0))
    ready(0, start)
    score(start, 0, 0)

    def serve_for(i):
        low = jnp.where(i <= 5, i, i + 1)
        high = jnp.where(i < 5, i, i + 1)

        def one(j, carry):
            serve(j, True)
            return carry

        lax.fori_loop(low, high + 1, one, 0)

    def step(i, carry):
        half = lax.rem(i, 2)
        now = pieces(i)
        for r in range(3):
            score(now, r + 1, (r + 1) % 2)
            mix(half, 4, r, r % 2)
        serve_for(i + 1)
        later = pieces(i + 1)
        ready(1 - half, later)
        score(later, 0, 0)
        mix(half, 4, 3, 1)
        return carry

    lax.fori_loop(0, 7, step, 0)

    now = pieces(jnp.int32(7))
    for r in range(3):
        score(now, r + 1, (r + 1) % 2)
        mix(1, 4, r, r % 2)
    end = [w_piece(-2), w_piece(3), (z, rank, z >= 0)]
    ready(0, end)
    turn = [lax.rem(y + 1 + j, 4) for j in range(4)]
    score(end, turn[0], 0, True)
    mix(1, 4, 3, 1)

    def o_copy(d):
        who = lax.rem(y + d, 4)
        return pltpu.make_async_remote_copy(
            src_ref=o_send.at[who],
            dst_ref=cut(out, y, G * D),
            send_sem=o_ssem.at[d - 1],
            recv_sem=o_rsem.at[d - 1],
            device_id=at_y(d),
            device_id_type=MESH,
        )

    own_out = pltpu.make_async_copy(o_send.at[y], cut(out, y, G * D), l_sem.at[3])
    for j in range(4):
        if j < 3:
            score(end, turn[j + 1], (j + 1) % 2, True)
        mix(0, 3, turn[j], j % 2)
        cols = block(turn[j])
        o = (acc[0:D, cols] * (1.0 / acc[D : D + 1, cols])).T.astype(BF)
        for h in range(G):
            o_send[turn[j], :, h * D : (h + 1) * D] = o[h * 64 : (h + 1) * 64, :]
        if j < 3:
            o_copy(j + 1).start()
        else:
            own_out.start()

    for kind in (0, 1, 2):
        for d in (1, 3, 2):
            y_copy(kind, d).wait_send()
    for j in range(4):

        @pl.when(core != j % 2)
        def _():
            x_copy(0, j).wait_send()

        for d in (1, 3, 2):
            x_copy(d, j).wait_send()

    def drain(j, carry):
        serve(j, False)
        return carry

    lax.fori_loop(0, 8, drain, 0)
    for d in (1, 2, 3):
        o_copy(d).wait_send()
    for d in (1, 2, 3):
        peer = lax.rem(y + 4 - d, 4)
        pltpu.make_async_remote_copy(
            src_ref=o_send.at[peer],
            dst_ref=cut(out, peer, G * D),
            send_sem=o_ssem.at[d - 1],
            recv_sem=o_rsem.at[d - 1],
            device_id=at_y(d),
            device_id_type=MESH,
        ).wait_recv()
    own_out.wait()


def body(queries, keys, values, doc_lengths):
    anywhere = pl.BlockSpec(memory_space=pl.ANY)
    dma = pltpu.SemaphoreType.DMA
    return pl.pallas_call(
        kernel,
        out_shape=jax.ShapeDtypeStruct(queries.shape, BF),
        in_specs=[pl.BlockSpec(memory_space=pltpu.SMEM), anywhere, anywhere, anywhere],
        out_specs=anywhere,
        scratch_shapes=[
            pltpu.VMEM((4, 64, G * D), BF),
            pltpu.VMEM((4, 64, 2 * D), BF),
            pltpu.VMEM((64, PIECE, 2 * D), BF),
            pltpu.VMEM((4 * ROWS, 2 * D), BF),
            pltpu.VMEM((4 * PIECE, D), BF),
            pltpu.VMEM((2, VR, 4 * PIECE), BF),
            pltpu.VMEM((VR, 4 * ROWS), F32),
            pltpu.VMEM((8, 4 * ROWS), F32),
            pltpu.VMEM((2, 4 * PIECE, ROWS), F32),
            pltpu.VMEM((2, 8, ROWS), F32),
            pltpu.VMEM((4, 64, G * D), BF),
            dma((3, 3)),
            dma((3, 3)),
            dma((4, 4)),
            dma((8, 4)),
            dma((3, 64)),
            dma((64,)),
            dma((3,)),
            dma((3,)),
            dma((4,)),
        ],
        compiler_params=pltpu.CompilerParams(
            collective_id=0, has_side_effects=True, vmem_limit_bytes=48 * 2**20
        ),
        cost_estimate=pl.CostEstimate(
            flops=12 * 10**9, bytes_accessed=10**7, transcendentals=18 * 10**6
        ),
    )(doc_lengths, queries, keys, values)


def solution(mesh):
    return jax.shard_map(
        body,
        mesh=mesh,
        in_specs=(P(("row", "col"), None), P(("col", "row"), None), P(("col", "row"), None), P()),
        out_specs=P(("row", "col"), None),
        check_vma=False,
    )
```

time: 735 us -> 123 us (0.17)
  the two profiles are of different devices: /device:TPU:8 before, /device:TPU:193 now
where the time goes in v1:
time: 123 us
  Pallas kernels  119 us (97%)
  local copies, waits for them, and re-layouts  4.17 us (3%)
    pallas_call x1, Pallas kernels, body(): pl.pallas_call(kernel, out_shape=jax.ShapeDtypeStruct(queries.shape, BF),...  119 us
    unnamed x9, local copies, waits for them, and re-layouts  4.17 us

profile of v1, /device:TPU:193, one launch (start us, length us, event | category | flops | bytes accessed | tf_op | source)
XLA Modules:
  0.0 123.3 jit_solution(7701747446173587885)
XLA Ops:
  0.0 0.0 copy-start
  0.0 1.0 copy-done
  1.0 0.0 copy-start.1
  1.0 0.8 copy-done.1
  1.9 0.0 copy-start.2
  1.9 0.8 copy-done.2
  2.7 0.0 copy-start.3
  2.7 0.7 copy-done.3
  3.4 119.1 %shard_map.46 = bf16[64,4096]{1,0:T(8,128)(2,1)S(1)} custom-call(s32[16]{0:T(128)S(1)} %copy-done.3, bf16[64,4096]{1,0:T(8,128)(2,1)S(1)} %copy-done, bf16[64,512]{1,0:T(8,128)(2,1)S(1)} %copy-done.1, bf16[64,512]{1,0:T(8,128)(2,1)S(1)} %copy-done.2), custom_call_target="tpu_custom_call" | custom-call | flops 12000000000 | bytes 10000000 | tf_op jit(solution)/shard_map/pallas_call | solution.py:435
  122.5 0.8 copy.6
Async XLA Ops:
  0.0 1.0 copy-start
  1.0 0.8 copy-start.1
  1.9 0.8 copy-start.2
  2.7 0.7 copy-start.3

commit v2 on v1

--- a/solution.py
+++ b/solution.py
@@ -41,6 +41,7 @@
     x_send,
     x_recv,
     c_send,
+    t_send,
     c_recv,
     o_ssem,
     o_rsem,
@@ -130,9 +131,12 @@
         total = total + lengths[d]
         doc_end = jnp.where(lane == d, total, doc_end)
 
-    def in_doc(start, count):
-        pos = start + lax.broadcasted_iota(jnp.int32, (count, D), 0)
+    def in_doc(offsets, start):
+        pos = start + offsets
         return (pos >= doc_first) & (pos < doc_end)
+
+    def spread(i):
+        return (i & 63) + ((i >> 6) & 1) * 128 + ((i >> 7) & 1) * 64
 
     pl.semaphore_wait(barrier, 12)
     for kind in (0, 1, 2):
@@ -145,48 +149,45 @@
         y_wait(0, d)
         y_wait(1, d)
 
-    def x_slot(chunk, who):
-        rows = pl.ds(pl.multiple_of(who * 64, 64), 64)
-        return kv.at[chunk * 8 + z, rows, :]
-
-    def x_copy(d, j):
+    def x_slot(chunk, half, who):
+        return kv.at[chunk * 8 + z, half, pl.ds(pl.multiple_of(who * 64, 64), 64), :]
+
+    def x_copy(n, j):
         chunk = x_lo * 4 + j
         return pltpu.make_async_remote_copy(
             src_ref=sub.at[j],
-            dst_ref=x_slot(chunk, x_hi * 2 + core),
-            send_sem=x_send.at[d, j],
-            recv_sem=x_recv.at[chunk, x_hi * 2 + core],
-            device_id=at_x(d, j % 2),
+            dst_ref=x_slot(chunk, core, x_hi),
+            send_sem=x_send.at[n, j],
+            recv_sem=x_recv.at[chunk, x_hi],
+            device_id=at_x(lax.rem(x_lo + core, 2) + 2 * n, j % 2),
             device_id_type=MESH,
         )
 
     def x_local(j):
         chunk = x_lo * 4 + j
         return pltpu.make_async_copy(
-            sub.at[j],
-            x_slot(chunk, x_hi * 2 + core),
-            x_recv.at[chunk, x_hi * 2 + core],
+            sub.at[j], x_slot(chunk, core, x_hi), x_recv.at[chunk, x_hi]
         )
 
     for j in range(4):
-
-        @pl.when(core == j % 2)
+        stays = (x_lo == core) & (core == j % 2)
+
+        @pl.when(stays)
         def _():
             x_local(j).start()
 
-        @pl.when(core != j % 2)
+        @pl.when(jnp.logical_not(stays))
         def _():
             x_copy(0, j).start()
 
-        for d in (1, 3, 2):
-            x_copy(d, j).start()
+        x_copy(1, j).start()
 
     own[2].wait()
     for d in (1, 3, 2):
         y_wait(2, d)
 
     for b in range(4):
-        seen = in_doc(first + b * 64, 64)
+        seen = in_doc(lax.broadcasted_iota(jnp.int32, (64, D), 0), first + b * 64)
         lanes = lax.broadcasted_iota(jnp.int32, (64, D), 1)
         wall = jnp.where(lanes < 16, jnp.where(seen, 0.0, HIDE), jnp.where(lanes == 16, HIDE, 0.0))
         wall = wall.astype(BF)
@@ -197,7 +198,7 @@
 
     def route(chunk):
         last = jnp.minimum(chunk + 4, 7)
-        before = jnp.where(chunk < 4, 1, 2)
+        before = 1 + lax.rem(chunk, 2)
         behind = jnp.maximum(chunk, 3) - before
         most_up = before + last - chunk
         most_down = behind + last - chunk
@@ -217,60 +218,141 @@
         paired = i <= 2 * both
         step = jnp.where(paired, (i + 1) // 2, i - both)
         rising = jnp.where(paired, lax.rem(i, 2) == 1, got_up > got_down)
-        return lax.rem(jnp.where(rising, z - step, z + step) + 8, 8), rising
-
-    def c_copy(way, piece):
+        return lax.rem(jnp.where(rising, z - step, z + step) + 8, 8)
+
+    def c_copy(way, half, piece, side=0):
+        who = (up, down, at_x(1 + 2 * side, core), twin)[way]
         return pltpu.make_async_remote_copy(
-            src_ref=kv.at[piece],
-            dst_ref=kv.at[piece],
-            send_sem=c_send.at[way, piece],
-            recv_sem=c_recv.at[piece],
-            device_id=(up, down, twin)[way],
+            src_ref=kv.at[piece, half],
+            dst_ref=kv.at[piece, half],
+            send_sem=t_send.at[half, piece] if way == 3 else c_send.at[way, piece],
+            recv_sem=c_recv.at[half, piece],
+            device_id=who,
             device_id_type=MESH,
         )
 
-    def serve(i, act):
-        def one(chunk, carry):
+    def pass_on(act, chunk, src, ways):
+        piece = chunk * 8 + src
+        side = lax.rem(chunk // 2 + src, 2)
+        for way, go in enumerate(ways):
+
+            @pl.when(go)
+            def _():
+                copy = c_copy(way, x_lo, piece, side)
+                if act:
+                    copy.start()
+                else:
+                    copy.wait_send()
+
+    def four(first_chunk, one):
+        def each(j, carry):
+            one(first_chunk + 2 * j)
+            return carry
+
+        lax.fori_loop(0, 4, each, 0)
+
+    def sides(t, got_up, got_down):
+        return (
+            (t <= got_up, lax.rem(z - t + 8, 8)),
+            (t <= got_down, lax.rem(z + t, 8)),
+        )
+
+    def chain_first(act):
+        def one(chunk):
+            _, _, on_up, on_down, wanted = route(chunk)
+            if act:
+                for who in range(2):
+                    pltpu.make_async_copy(
+                        sub.at[0], x_slot(chunk, x_lo, who), x_recv.at[chunk, who]
+                    ).wait()
+            pass_on(act, chunk, z, (on_up, on_down, wanted, wanted))
+
+        four(core, one)
+
+    def chain(t, act):
+        def one(chunk):
             got_up, got_down, on_up, on_down, wanted = route(chunk)
-            src, rising = source(got_up, got_down, i)
-            src = jnp.where(i == 0, z, src)
-            piece = chunk * 8 + src
-            mine = lax.rem(chunk, 2) == core
-            there = i <= got_up + got_down
-            go_up = mine & there & on_up & ((i == 0) | rising)
-            go_down = mine & there & on_down & ((i == 0) | jnp.logical_not(rising))
-            go_twin = mine & there & wanted
-            if act:
-
-                @pl.when(mine & (i == 0))
-                def _():
-                    for who in range(4):
-                        pltpu.make_async_copy(
-                            sub.at[0], x_slot(chunk, who), x_recv.at[chunk, who]
-                        ).wait()
-
-                @pl.when(there & ((mine & (i > 0)) | (jnp.logical_not(mine) & wanted)))
-                def _():
-                    c_copy(0, piece).wait_recv()
-
-            for way, go in ((0, go_up), (1, go_down), (2, go_twin)):
-
-                @pl.when(go)
+            up_side, down_side = sides(t, got_up, got_down)
+            for (there, src), ways in (
+                (up_side, (on_up, None)),
+                (down_side, (None, on_down)),
+            ):
+
+                @pl.when(there)
                 def _():
                     if act:
-                        c_copy(way, piece).start()
+                        c_copy(3, x_lo, chunk * 8 + src).wait_recv()
+                    never = chunk < 0
+                    pass_on(
+                        act,
+                        chunk,
+                        src,
+                        tuple(never if w is None else w for w in ways) + (wanted, wanted),
+                    )
+
+        four(core, one)
+
+    def across(t, act):
+        def one(chunk):
+            got_up, got_down, _, _, wanted = route(chunk)
+            for there, src in sides(t, got_up, got_down):
+
+                @pl.when(there & wanted)
+                def _():
+                    copy = c_copy(3, 1 - x_lo, chunk * 8 + src)
+                    if act:
+                        copy.wait_recv()
+                        copy.start()
                     else:
-                        c_copy(way, piece).wait_send()
-
-            return carry
-
-        lax.fori_loop(0, 8, one, 0)
+                        copy.wait_send()
+
+        four(core, one)
+
+    def across_first(act):
+        def one(chunk):
+            wanted = route(chunk)[4]
+
+            @pl.when(wanted)
+            def _():
+                copy = c_copy(3, 1 - x_lo, chunk * 8 + z)
+                if act:
+                    copy.wait_recv()
+                    copy.start()
+                else:
+                    copy.wait_send()
+
+        four(core, one)
+
+    def from_twin(t):
+        def one(chunk):
+            got_up, got_down, _, _, wanted = route(chunk)
+            for there, src in sides(t, got_up, got_down):
+
+                @pl.when(there & wanted)
+                def _():
+                    for half in range(2):
+                        c_copy(3, half, chunk * 8 + src).wait_recv()
+
+        four(1 - core, one)
+
+    def from_twin_first():
+        def one(chunk):
+            wanted = route(chunk)[4]
+
+            @pl.when(wanted)
+            def _():
+                for half in range(2):
+                    c_copy(3, half, chunk * 8 + z).wait_recv()
+
+        four(1 - core, one)
 
     def w_piece(step):
         src = lax.rem(z + step + 8, 8)
         chunk = jnp.where(src < rank, z, z - 4)
         live = chunk >= 0
         return jnp.where(live, chunk, z), jnp.where(live, src, z), live
+
+    near = jnp.where(lax.rem(z, 2) == 0, 2, -2)
 
     def pieces(i):
         got = []
@@ -278,40 +360,39 @@
             chunk = z - back
             live = chunk >= 0
             got_up, got_down, _, _, _ = route(jnp.maximum(chunk, 0))
-            src, _ = source(got_up, got_down, i)
-            src = jnp.where(i == 0, z, src)
+            src = jnp.where(i == 0, z, source(got_up, got_down, i))
             got.append((jnp.where(live, chunk, z), jnp.where(live, src, z), live))
         step = jnp.where(i == 1, -1, 0)
-        step = jnp.where(i == 2, 1, step)
-        step = jnp.where(i == 4, 2, step)
-        step = jnp.where(i == 6, 4, step)
-        step = jnp.where(i == 7, -3, step)
-        chunk, src, live = w_piece(step)
-        got.append((chunk, src, live & (i != 3) & (i != 5)))
+        for at, value in ((2, 1), (3, near), (4, 4), (5, 3), (6, -3), (7, -near)):
+            step = jnp.where(i == at, value, step)
+        got.append(w_piece(step))
         return got
 
     def ready(half, got):
         for n, (chunk, src, live) in enumerate(got):
             piece = chunk * 8 + src
             at = slice(n * PIECE, (n + 1) * PIECE)
-            vt[half, 0:D, at] = kv[piece, :, D : 2 * D].T
-            seen = in_doc(chunk * 2048 + src * 256, PIECE)
+            vt[half, 0:D, at] = kv[piece, :, :, D : 2 * D].reshape(PIECE, D).T
+            seen = in_doc(spread(lax.broadcasted_iota(jnp.int32, (PIECE, D), 0)), chunk * 2048 + src * 256)
             lanes = lax.broadcasted_iota(jnp.int32, (PIECE, D), 1)
             flag = jnp.where(live, jnp.where(seen, 1.0, 0.0), jnp.where(lanes == 16, 1.0, 0.0))
-            kd[at, :] = flag.astype(BF)
+            kd[half, at, :] = flag.astype(BF)
+
+    turn = [lax.rem(y + 1 + j, 4) for j in range(4)]
 
     def block(r):
         return pl.ds(pl.multiple_of(r * ROWS, ROWS), ROWS)
 
-    def score(got, r, slot, diagonal=False):
+    def score(half, got, r, slot, diagonal=False):
         q = q_aug[block(r), :]
         best = None
         for n, (chunk, src, _) in enumerate(got):
             at = slice(n * PIECE, (n + 1) * PIECE)
-            k = jnp.concatenate([kv[chunk * 8 + src, :, 0:D], kd[at, :]], axis=1)
+            k = kv[chunk * 8 + src, :, :, 0:D].reshape(PIECE, D)
+            k = jnp.concatenate([k, kd[half, at, :]], axis=1)
             s = lax.dot_general(k, q, (((1,), (1,)), ((), ())), preferred_element_type=F32)
-            if diagonal and n == len(got) - 1:
-                key = lax.broadcasted_iota(jnp.int32, (PIECE, ROWS), 0)
+            if diagonal:
+                key = spread(lax.broadcasted_iota(jnp.int32, (PIECE, ROWS), 0))
                 query = r * 64 + (lax.broadcasted_iota(jnp.int32, (PIECE, ROWS), 1) & 63)
                 s = jnp.where(key <= query, s, HIDE)
             sb[slot, at, :] = s
@@ -332,45 +413,37 @@
         acc[:, cols] = sums
         top[0:1, cols] = new
 
-    serve(jnp.int32(0), True)
+    chain_first(True)
+    chain(jnp.int32(1), True)
+    across_first(True)
+    from_twin_first()
     start = pieces(jnp.int32(0))
     ready(0, start)
-    score(start, 0, 0)
-
-    def serve_for(i):
-        low = jnp.where(i <= 5, i, i + 1)
-        high = jnp.where(i < 5, i, i + 1)
-
-        def one(j, carry):
-            serve(j, True)
-            return carry
-
-        lax.fori_loop(low, high + 1, one, 0)
+    score(0, start, turn[0], 0)
 
     def step(i, carry):
         half = lax.rem(i, 2)
         now = pieces(i)
-        for r in range(3):
-            score(now, r + 1, (r + 1) % 2)
-            mix(half, 4, r, r % 2)
-        serve_for(i + 1)
+        score(half, now, turn[1], 1)
+        mix(half, 4, turn[0], 0)
+        score(half, now, turn[2], 0)
+        mix(half, 4, turn[1], 1)
+        chain(i + 2, True)
+        across(i + 1, True)
+        score(half, now, turn[3], 1)
+        mix(half, 4, turn[2], 0)
+        from_twin(i + 1)
         later = pieces(i + 1)
         ready(1 - half, later)
-        score(later, 0, 0)
-        mix(half, 4, 3, 1)
+        score(1 - half, later, turn[0], 0)
+        mix(half, 4, turn[3], 1)
         return carry
 
     lax.fori_loop(0, 7, step, 0)
 
     now = pieces(jnp.int32(7))
-    for r in range(3):
-        score(now, r + 1, (r + 1) % 2)
-        mix(1, 4, r, r % 2)
-    end = [w_piece(-2), w_piece(3), (z, rank, z >= 0)]
+    end = [(z, rank, z >= 0)]
     ready(0, end)
-    turn = [lax.rem(y + 1 + j, 4) for j in range(4)]
-    score(end, turn[0], 0, True)
-    mix(1, 4, 3, 1)
 
     def o_copy(d):
         who = lax.rem(y + d, 4)
@@ -385,9 +458,11 @@
 
     own_out = pltpu.make_async_copy(o_send.at[y], cut(out, y, G * D), l_sem.at[3])
     for j in range(4):
+        score(0, end, turn[j], 1, True)
+        mix(1, 4, turn[j], 0)
         if j < 3:
-            score(end, turn[j + 1], (j + 1) % 2, True)
-        mix(0, 3, turn[j], j % 2)
+            score(1, now, turn[j + 1], 0)
+        mix(0, 1, turn[j], 1)
         cols = block(turn[j])
         o = (acc[0:D, cols] * (1.0 / acc[D : D + 1, cols])).T.astype(BF)
         for h in range(G):
@@ -402,18 +477,21 @@
             y_copy(kind, d).wait_send()
     for j in range(4):
 
-        @pl.when(core != j % 2)
+        @pl.when(jnp.logical_not((x_lo == core) & (core == j % 2)))
         def _():
             x_copy(0, j).wait_send()
 
-        for d in (1, 3, 2):
-            x_copy(d, j).wait_send()
-
-    def drain(j, carry):
-        serve(j, False)
+        x_copy(1, j).wait_send()
+
+    chain_first(False)
+    across_first(False)
+
+    def drain(t, carry):
+        chain(t, False)
+        across(t, False)
         return carry
 
-    lax.fori_loop(0, 8, drain, 0)
+    lax.fori_loop(1, 7, drain, 0)
     for d in (1, 2, 3):
         o_copy(d).wait_send()
     for d in (1, 2, 3):
@@ -431,18 +509,19 @@
 
 def body(queries, keys, values, doc_lengths):
     anywhere = pl.BlockSpec(memory_space=pl.ANY)
+    hbm = pl.BlockSpec(memory_space=pltpu.HBM)
     dma = pltpu.SemaphoreType.DMA
     return pl.pallas_call(
         kernel,
         out_shape=jax.ShapeDtypeStruct(queries.shape, BF),
-        in_specs=[pl.BlockSpec(memory_space=pltpu.SMEM), anywhere, anywhere, anywhere],
+        in_specs=[pl.BlockSpec(memory_space=pltpu.SMEM), hbm, hbm, hbm],
         out_specs=anywhere,
         scratch_shapes=[
             pltpu.VMEM((4, 64, G * D), BF),
             pltpu.VMEM((4, 64, 2 * D), BF),
-            pltpu.VMEM((64, PIECE, 2 * D), BF),
+            pltpu.VMEM((64, 2, PIECE // 2, 2 * D), BF),
             pltpu.VMEM((4 * ROWS, 2 * D), BF),
-            pltpu.VMEM((4 * PIECE, D), BF),
+            pltpu.VMEM((2, 4 * PIECE, D), BF),
             pltpu.VMEM((2, VR, 4 * PIECE), BF),
             pltpu.VMEM((VR, 4 * ROWS), F32),
             pltpu.VMEM((8, 4 * ROWS), F32),
@@ -451,16 +530,17 @@
             pltpu.VMEM((4, 64, G * D), BF),
             dma((3, 3)),
             dma((3, 3)),
-            dma((4, 4)),
-            dma((8, 4)),
+            dma((2, 4)),
+            dma((8, 2)),
             dma((3, 64)),
-            dma((64,)),
+            dma((2, 64)),
+            dma((2, 64)),
             dma((3,)),
             dma((3,)),
             dma((4,)),
         ],
         compiler_params=pltpu.CompilerParams(
-            collective_id=0, has_side_effects=True, vmem_limit_bytes=48 * 2**20
+            collective_id=0, has_side_effects=True, vmem_limit_bytes=60 * 2**20
         ),
         cost_estimate=pl.CostEstimate(
             flops=12 * 10**9, bytes_accessed=10**7, transcendentals=18 * 10**6

time: 123 us -> 69.6 us (0.57)
  the two profiles are of different devices: /device:TPU:193 before, /device:TPU:8 now
where the time goes in v2:
time: 69.6 us; the launch traced here: 68.2 us
  Pallas kernels  66.3 us (95%)
  local copies, waits for them, and re-layouts  1.87 us (3%)
    pallas_call x1, Pallas kernels, body(): pl.pallas_call(kernel, out_shape=jax.ShapeDtypeStruct(queries.shape, BF),...  66.3 us
    unnamed x1, local copies, waits for them, and re-layouts  1.87 us

profile of v2, /device:TPU:8, one launch (start us, length us, event | category | flops | bytes accessed | tf_op | source)
XLA Modules:
  0.0 68.2 jit_solution(18139017136714827188)
XLA Ops:
  0.0 66.3 %shard_map.46 = bf16[64,4096]{1,0:T(8,128)(2,1)} custom-call(s32[16]{0:T(128)} %lengths.1, bf16[64,4096]{1,0:T(8,128)(2,1)} %queries.1, bf16[64,512]{1,0:T(8,128)(2,1)} %keys.1, bf16[64,512]{1,0:T(8,128)(2,1)} %values.1), custom_call_target="tpu_custom_call" | custom-call | flops 12000000000 | bytes 10000000 | tf_op jit(solution)/shard_map/pallas_call | solution.py:514
  66.3 1.9 %copy.6 = bf16[64,4096]{1,0:T(8,128)(2,1)} copy(bf16[64,4096]{1,0:T(8,128)(2,1)} %shard_map.46) | data formatting | bytes 1048576

commit v3 on v2

v3 whole, which is shorter than its diff:
```python
import jax
import jax.numpy as jnp
from jax import lax
from jax.experimental import pallas as pl
from jax.experimental.pallas import tpu as pltpu
from jax.sharding import PartitionSpec as P

D = 128
G = 8
BF = jnp.bfloat16
F32 = jnp.float32
LOG2E = 1.4426950408889634
SCALE = LOG2E / D**0.5
HIDE = -1e30
FLOOR = -3e30
PIECE = 256
ROWS = 512
VR = 144
MESH = pl.DeviceIdType.MESH


def kernel(
    lengths,
    queries,
    keys,
    values,
    out,
    q_in,
    kv,
    q_aug,
    kd,
    vt,
    acc,
    top,
    sb,
    mb,
    o_send,
    k_send,
    k_recv,
    q_send,
    q_recv,
    c_send,
    c_recv,
    x_recv,
    t_send,
    t_recv,
    o_ssem,
    o_rsem,
    l_sem,
):
    row = lax.axis_index("row")
    col = lax.axis_index("col")
    z = row // 4
    x_hi = (row // 2) % 2
    core = row % 2
    x_lo = col // 4
    y = col % 4
    x = x_hi * 2 + x_lo
    rank = x_hi * 4 + core * 2 + x_lo
    first = z * 2048 + rank * 256
    up = (lax.rem(row + 4, 32), col)
    down = (lax.rem(row + 28, 32), col)
    twin = (row + 1 - 2 * core, col)

    def at_y(d):
        return (row, x_lo * 4 + lax.rem(y + d, 4))

    def at_x(d, k):
        xd = lax.rem(x + d, 4)
        return (z * 4 + (xd // 2) * 2 + k, (xd % 2) * 4 + y)

    selfish = (lax.rem(y, 2) == core) & (core == x_lo)

    barrier = pltpu.get_barrier_semaphore()

    def greet(who):
        pl.semaphore_signal(barrier, inc=1, device_id=who, device_id_type=MESH)

    for who in (twin, up, down, at_x(1, core), at_x(3, core), at_y(1), at_y(2), at_y(3)):
        greet(who)
    for j in range(4):
        chunk = core + 2 * j
        for n in range(2):
            who = (z * 4 + n * 2 + x_lo, chunk)

            @pl.when(jnp.logical_not(selfish & (n == x_hi) & (chunk == col)))
            def _():
                greet(who)

    def cut(ref, head, width):
        return ref.at[:, pl.ds(pl.multiple_of(head * width, width), width)]

    def slot(kind, chunk, half, who):
        rows = pl.ds(pl.multiple_of(who * 64, 64), 64)
        return kv.at[chunk * 8 + z, half, rows, kind * D : (kind + 1) * D]

    def k_copy(kind, n, d):
        head = lax.rem(y + d, 4)
        return pltpu.make_async_remote_copy(
            src_ref=cut((keys, values)[kind], head, D),
            dst_ref=slot(kind, col, core, x_hi),
            send_sem=k_send.at[kind, n, d],
            recv_sem=k_recv.at[kind, col, x_hi],
            device_id=(z * 4 + n * 2 + lax.rem(y, 2), core * 4 + head),
            device_id_type=MESH,
        )

    def k_local(kind):
        return pltpu.make_async_copy(
            cut((keys, values)[kind], y, D),
            slot(kind, col, core, x_hi),
            k_recv.at[kind, col, x_hi],
        )

    def k_each(act):
        for d in (1, 3, 2, 0):
            for n in range(2):

                def one():
                    for kind in range(2):
                        copy = k_copy(kind, n, d)
                        if act:
                            copy.start()
                        else:
                            copy.wait_send()

                if d == 0:
                    pl.when(jnp.logical_not(selfish & (n == x_hi)))(one)
                else:
                    one()

    own_q = pltpu.make_async_copy(cut(queries, y, G * D), q_in.at[y], l_sem.at[0])

    def q_copy(d):
        return pltpu.make_async_remote_copy(
            src_ref=cut(queries, lax.rem(y + d, 4), G * D),
            dst_ref=q_in.at[y],
            send_sem=q_send.at[d - 1],
            recv_sem=q_recv.at[d - 1],
            device_id=at_y(d),
            device_id_type=MESH,
        )

    def q_wait(d):
        dst = q_in.at[lax.rem(y + 4 - d, 4)]
        pltpu.make_async_remote_copy(
            src_ref=dst,
            dst_ref=dst,
            send_sem=q_send.at[d - 1],
            recv_sem=q_recv.at[d - 1],
            device_id=at_y(d),
            device_id_type=MESH,
        ).wait_recv()

    own_q.start()

    @pl.when(selfish)
    def _():
        for kind in range(2):
            k_local(kind).start()

    acc[...] = jnp.zeros_like(acc)
    top[...] = jnp.full_like(top, FLOOR)
    vt[:, D:VR, :] = jnp.ones((2, VR - D, 5 * PIECE), BF)

    lane = lax.broadcasted_iota(jnp.int32, (1, D), 1)
    doc_first = jnp.zeros((1, D), jnp.int32)
    doc_end = jnp.zeros((1, D), jnp.int32)
    total = jnp.int32(0)
    for d in range(16):
        doc_first = jnp.where(lane == d, total, doc_first)
        total = total + lengths[d]
        doc_end = jnp.where(lane == d, total, doc_end)

    def in_doc(offsets, start):
        pos = start + offsets
        return (pos >= doc_first) & (pos < doc_end)

    def spread(i):
        return (i & 63) + ((i >> 6) & 1) * 128 + ((i >> 7) & 1) * 64

    pl.semaphore_wait(barrier, 16 - jnp.where(selfish, 1, 0))
    k_each(True)
    for d in (1, 3, 2):
        q_copy(d).start()

    def build(b):
        offsets = lax.broadcasted_iota(jnp.int32, (64, D), 0)
        seen = in_doc(offsets, first + b * 64)
        lanes = lax.broadcasted_iota(jnp.int32, (64, D), 1)
        wall = jnp.where(lanes < 16, jnp.where(seen, 0.0, HIDE), jnp.where(lanes == 16, HIDE, 0.0))
        wall = wall.astype(BF)
        for h in range(G):
            at = pl.ds(pl.multiple_of((b * G + h) * 64, 64), 64)
            q_aug[at, 0:D] = q_in[b, :, h * D : (h + 1) * D]
            q_aug[at, D : 2 * D] = wall

    def route(chunk):
        last = jnp.minimum(chunk + 4, 7)
        before = 1 + lax.rem(chunk, 2)
        behind = jnp.maximum(chunk, 3) - before
        most_up = before + last - chunk
        most_down = behind + last - chunk
        u = lax.rem(z - chunk + before + 16, 8)
        v = lax.rem(last + behind - z + 16, 8)
        in_up = u <= most_up
        in_down = v <= most_down
        got_up = jnp.where(in_up, u, 0)
        got_down = jnp.where(in_down, v, 0)
        on_up = in_up & (u < most_up)
        on_down = in_down & (v < most_down)
        wanted = (z >= chunk) & (z <= chunk + 4)
        return got_up, got_down, on_up, on_down, wanted

    def source(got_up, got_down, i):
        both = jnp.minimum(got_up, got_down)
        paired = i <= 2 * both
        step = jnp.where(paired, (i + 1) // 2, i - both)
        rising = jnp.where(paired, lax.rem(i, 2) == 1, got_up > got_down)
        return lax.rem(jnp.where(rising, z - step, z + step) + 8, 8)

    mine = [(core + 2 * j, route(core + 2 * j)) for j in range(4)]
    theirs = [(1 - core + 2 * j, route(1 - core + 2 * j)) for j in range(4)]

    def c_copy(way, piece, side=0):
        who = (up, down, at_x(1 + 2 * side, core))[way]
        return pltpu.make_async_remote_copy(
            src_ref=kv.at[piece, x_lo],
            dst_ref=kv.at[piece, x_lo],
            send_sem=c_send.at[way, piece],
            recv_sem=c_recv.at[piece],
            device_id=who,
            device_id_type=MESH,
        )

    def x_arrival(piece):
        return pltpu.make_async_remote_copy(
            src_ref=kv.at[piece, 1 - x_lo],
            dst_ref=kv.at[piece, 1 - x_lo],
            send_sem=c_send.at[2, piece],
            recv_sem=x_recv.at[piece],
            device_id=up,
            device_id_type=MESH,
        )

    def x_copy(piece, side):
        return pltpu.make_async_remote_copy(
            src_ref=kv.at[piece, x_lo],
            dst_ref=kv.at[piece, x_lo],
            send_sem=c_send.at[2, piece],
            recv_sem=x_recv.at[piece],
            device_id=at_x(1 + 2 * side, core),
            device_id_type=MESH,
        )

    def t_copy(piece):
        return pltpu.make_async_remote_copy(
            src_ref=kv.at[piece],
            dst_ref=kv.at[piece],
            send_sem=t_send.at[piece],
            recv_sem=t_recv.at[piece],
            device_id=twin,
            device_id_type=MESH,
        )

    def do(act, copy):
        if act:
            copy.start()
        else:
            copy.wait_send()

    def spread_x(act, chunk, src):
        do(act, x_copy(chunk * 8 + src, lax.rem(chunk // 2 + src, 2)))

    def sides(t, got_up, got_down):
        return (
            (t <= got_up, lax.rem(z - t + 8, 8)),
            (t <= got_down, lax.rem(z + t, 8)),
        )

    def chain_first(act):
        for chunk, (_, _, on_up, on_down, wanted) in mine:
            if act:
                for who in range(2):
                    for kind in range(2):
                        pltpu.make_async_copy(
                            slot(kind, chunk, x_lo, who),
                            slot(kind, chunk, x_lo, who),
                            k_recv.at[kind, chunk, who],
                        ).wait()
            piece = chunk * 8 + z

            @pl.when(on_up)
            def _():
                do(act, c_copy(0, piece))

            @pl.when(on_down)
            def _():
                do(act, c_copy(1, piece))

            @pl.when(wanted)
            def _():
                spread_x(act, chunk, z)

    def chain(t, act):
        for chunk, (got_up, got_down, on_up, on_down, wanted) in mine:
            for way, (there, src) in enumerate(sides(t, got_up, got_down)):

                @pl.when(there)
                def _():
                    piece = chunk * 8 + src
                    if act:
                        c_copy(way, piece).wait_recv()

                    @pl.when((on_up, on_down)[way])
                    def _():
                        do(act, c_copy(way, piece))

                    @pl.when(wanted)
                    def _():
                        spread_x(act, chunk, src)

    def across(t, act):
        for chunk, (got_up, got_down, _, _, wanted) in mine:
            for there, src in sides(t, got_up, got_down):

                @pl.when(there & wanted)
                def _():
                    piece = chunk * 8 + src
                    if act:
                        x_arrival(piece).wait_recv()
                    do(act, t_copy(piece))

    def across_first(act):
        for chunk, route_of in mine:

            @pl.when(route_of[4])
            def _():
                piece = chunk * 8 + z
                if act:
                    x_arrival(piece).wait_recv()
                do(act, t_copy(piece))

    def from_twin(t):
        for chunk, (got_up, got_down, _, _, wanted) in theirs:
            for there, src in sides(t, got_up, got_down):

                @pl.when(there & wanted)
                def _():
                    t_copy(chunk * 8 + src).wait_recv()

    def from_twin_first():
        for chunk, route_of in theirs:

            @pl.when(route_of[4])
            def _():
                t_copy(chunk * 8 + z).wait_recv()

    def w_piece(step):
        src = lax.rem(z + step + 8, 8)
        chunk = jnp.where(src < rank, z, z - 4)
        live = chunk >= 0
        return jnp.where(live, chunk, z), jnp.where(live, src, z), live

    near = jnp.where(lax.rem(z, 2) == 0, 2, -2)

    def pieces(i):
        got = []
        for back in (3, 2, 1):
            chunk = z - back
            live = chunk >= 0
            got_up, got_down, _, _, _ = route(jnp.maximum(chunk, 0))
            src = jnp.where(i == 0, z, source(got_up, got_down, i))
            got.append((jnp.where(live, chunk, z), jnp.where(live, src, z), live))
        step = jnp.where(i == 1, -1, 0)
        for at, value in ((2, 1), (3, near), (4, 4), (5, 3), (6, -3), (7, -near)):
            step = jnp.where(i == at, value, step)
        got.append(w_piece(step))
        return got

    def ready(half, got):
        for n, (chunk, src, live) in enumerate(got):
            piece = chunk * 8 + src
            at = slice(n * PIECE, (n + 1) * PIECE)
            vt[half, 0:D, at] = kv[piece, :, :, D : 2 * D].reshape(PIECE, D).T
            seen = in_doc(spread(lax.broadcasted_iota(jnp.int32, (PIECE, D), 0)), chunk * 2048 + src * 256)
            lanes = lax.broadcasted_iota(jnp.int32, (PIECE, D), 1)
            flag = jnp.where(live, jnp.where(seen, 1.0, 0.0), jnp.where(lanes == 16, 1.0, 0.0))
            kd[half, at, :] = flag.astype(BF)

    turn = [lax.rem(y + 1 + j, 4) for j in range(4)]

    def block(r):
        return pl.ds(pl.multiple_of(r * ROWS, ROWS), ROWS)

    def score(half, got, r, slot):
        q = q_aug[block(r), :]
        best = None
        for n, (chunk, src, *_) in enumerate(got):
            at = slice(n * PIECE, (n + 1) * PIECE)
            k = kv[chunk * 8 + src, :, :, 0:D].reshape(PIECE, D)
            k = jnp.concatenate([k, kd[half, at, :]], axis=1)
            s = lax.dot_general(k, q, (((1,), (1,)), ((), ())), preferred_element_type=F32)
            if n == 4:
                key = spread(lax.broadcasted_iota(jnp.int32, (PIECE, ROWS), 0))
                query = r * 64 + (lax.broadcasted_iota(jnp.int32, (PIECE, ROWS), 1) & 63)
                s = jnp.where(key <= query, s, HIDE)
            sb[slot, at, :] = s
            here = jnp.max(s, axis=0, keepdims=True)
            best = here if best is None else jnp.maximum(best, here)
        mb[slot, 0:1, :] = best

    def mix(half, count, r, slot):
        cols = block(r)
        old = top[0:1, cols]
        new = jnp.maximum(old, mb[slot, 0:1, :])
        shift = new * SCALE
        sums = acc[:, cols] * jnp.exp2((old - new) * SCALE)
        for n in range(count):
            at = slice(n * PIECE, (n + 1) * PIECE)
            w = jnp.exp2(sb[slot, at, :] * SCALE - shift).astype(BF)
            sums = sums + jnp.dot(vt[half, :, at], w, preferred_element_type=F32)
        acc[:, cols] = sums
        top[0:1, cols] = new

    chain_first(True)
    own_q.wait()
    build(y)
    for d in (1, 3, 2):
        q_wait(d)
        build(lax.rem(y + 4 - d, 4))
    chain(1, True)
    across_first(True)
    from_twin_first()
    start = pieces(jnp.int32(0))
    ready(0, start)
    score(0, start, turn[0], 0)

    def step(i, carry):
        half = lax.rem(i, 2)
        now = pieces(i)
        score(half, now, turn[1], 1)
        mix(half, 4, turn[0], 0)
        score(half, now, turn[2], 0)
        mix(half, 4, turn[1], 1)
        chain(i + 2, True)
        across(i + 1, True)
        score(half, now, turn[3], 1)
        mix(half, 4, turn[2], 0)
        from_twin(i + 1)
        later = pieces(i + 1)
        ready(1 - half, later)
        score(1 - half, later, turn[0], 0)
        mix(half, 4, turn[3], 1)
        return carry

    lax.fori_loop(0, 6, step, 0)

    now = pieces(jnp.int32(6))
    end = pieces(jnp.int32(7)) + [(z, rank, z >= 0)]
    ready(1, end)

    def o_copy(d):
        who = lax.rem(y + d, 4)
        return pltpu.make_async_remote_copy(
            src_ref=o_send.at[who],
            dst_ref=cut(out, y, G * D),
            send_sem=o_ssem.at[d - 1],
            recv_sem=o_rsem.at[d - 1],
            device_id=at_y(d),
            device_id_type=MESH,
        )

    own_out = pltpu.make_async_copy(o_send.at[y], cut(out, y, G * D), l_sem.at[1])
    for j in range(4):
        score(1, end, turn[j], 1)
        mix(0, 4, turn[j], 0)
        if j < 3:
            score(0, now, turn[j + 1], 0)
        mix(1, 5, turn[j], 1)
        cols = block(turn[j])
        o = (acc[0:D, cols] * (1.0 / acc[D : D + 1, cols])).T.astype(BF)
        for h in range(G):
            o_send[turn[j], :, h * D : (h + 1) * D] = o[h * 64 : (h + 1) * 64, :]
        if j < 3:
            o_copy(j + 1).start()
        else:
            own_out.start()

    k_each(False)
    for d in (1, 3, 2):
        q_copy(d).wait_send()
    chain_first(False)
    across_first(False)

    def drain(t, carry):
        chain(t, False)
        across(t, False)
        return carry

    lax.fori_loop(1, 7, drain, 0)
    for d in (1, 2, 3):
        o_copy(d).wait_send()
    for d in (1, 2, 3):
        peer = lax.rem(y + 4 - d, 4)
        pltpu.make_async_remote_copy(
            src_ref=o_send.at[peer],
            dst_ref=cut(out, peer, G * D),
            send_sem=o_ssem.at[d - 1],
            recv_sem=o_rsem.at[d - 1],
            device_id=at_y(d),
            device_id_type=MESH,
        ).wait_recv()
    own_out.wait()


def body(queries, keys, values, doc_lengths):
    anywhere = pl.BlockSpec(memory_space=pl.ANY)
    hbm = pl.BlockSpec(memory_space=pltpu.HBM)
    dma = pltpu.SemaphoreType.DMA
    return pl.pallas_call(
        kernel,
        out_shape=jax.ShapeDtypeStruct(queries.shape, BF),
        in_specs=[pl.BlockSpec(memory_space=pltpu.SMEM), hbm, hbm, hbm],
        out_specs=anywhere,
        scratch_shapes=[
            pltpu.VMEM((4, 64, G * D), BF),
            pltpu.VMEM((64, 2, PIECE // 2, 2 * D), BF),
            pltpu.VMEM((4 * ROWS, 2 * D), BF),
            pltpu.VMEM((2, 5 * PIECE, D), BF),
            pltpu.VMEM((2, VR, 5 * PIECE), BF),
            pltpu.VMEM((VR, 4 * ROWS), F32),
            pltpu.VMEM((8, 4 * ROWS), F32),
            pltpu.VMEM((2, 5 * PIECE, ROWS), F32),
            pltpu.VMEM((2, 8, ROWS), F32),
            pltpu.VMEM((4, 64, G * D), BF),
            dma((2, 2, 4)),
            dma((2, 8, 2)),
            dma((3,)),
            dma((3,)),
            dma((3, 64)),
            dma((64,)),
            dma((64,)),
            dma((64,)),
            dma((64,)),
            dma((3,)),
            dma((3,)),
            dma((2,)),
        ],
        compiler_params=pltpu.CompilerParams(
            collective_id=0, has_side_effects=True, vmem_limit_bytes=60 * 2**20
        ),
        cost_estimate=pl.CostEstimate(
            flops=12 * 10**9, bytes_accessed=10**7, transcendentals=18 * 10**6
        ),
    )(doc_lengths, queries, keys, values)


def solution(mesh):
    return jax.shard_map(
        body,
        mesh=mesh,
        in_specs=(P(("row", "col"), None), P(("col", "row"), None), P(("col", "row"), None), P()),
        out_specs=P(("row", "col"), None),
        check_vma=False,
    )
```

time: 69.6 us -> 65.4 us (0.940); the launches traced: 68.2 us -> 65.1 us
  Pallas kernels: 66.3 us -> 63.2 us
    pallas_call x1, Pallas kernels: 66.3 us -> 63.2 us  [body(): pl.pallas_call(kernel, out_shape=jax.ShapeDtypeStruct(queries.shape, BF),...]
where the time goes in v3:
time: 65.4 us; the launch traced here: 65.1 us
  Pallas kernels  63.2 us (97%)
  local copies, waits for them, and re-layouts  1.87 us (3%)
    pallas_call x1, Pallas kernels, body(): pl.pallas_call(kernel, out_shape=jax.ShapeDtypeStruct(queries.shape, BF),...  63.2 us
    unnamed x1, local copies, waits for them, and re-layouts  1.87 us

profile of v3, /device:TPU:8, one launch (start us, length us, event | category | flops | bytes accessed | tf_op | source)
XLA Modules:
  0.0 65.1 jit_solution(8780415181402922832)
XLA Ops:
  0.0 63.2 %shard_map.46 = bf16[64,4096]{1,0:T(8,128)(2,1)} custom-call(s32[16]{0:T(128)} %lengths.1, bf16[64,4096]{1,0:T(8,128)(2,1)} %queries.1, bf16[64,512]{1,0:T(8,128)(2,1)} %keys.1, bf16[64,512]{1,0:T(8,128)(2,1)} %values.1), custom_call_target="tpu_custom_call" | custom-call | flops 12000000000 | bytes 10000000 | tf_op jit(solution)/shard_map/pallas_call | solution.py:521
  63.2 1.9 %copy.6 = bf16[64,4096]{1,0:T(8,128)(2,1)} copy(bf16[64,4096]{1,0:T(8,128)(2,1)} %shard_map.46) | data formatting | bytes 1048576

commit v4 on v3

--- a/solution.py
+++ b/solution.py
@@ -26,6 +26,8 @@
     values,
     out,
     q_in,
+    q_out,
+    k_out,
     kv,
     q_aug,
     kd,
@@ -47,6 +49,7 @@
     o_ssem,
     o_rsem,
     l_sem,
+    s_sem,
 ):
     row = lax.axis_index("row")
     col = lax.axis_index("col")
@@ -90,50 +93,63 @@
     def cut(ref, head, width):
         return ref.at[:, pl.ds(pl.multiple_of(head * width, width), width)]
 
-    def slot(kind, chunk, half, who):
+    def slot(chunk, half, who):
         rows = pl.ds(pl.multiple_of(who * 64, 64), 64)
-        return kv.at[chunk * 8 + z, half, rows, kind * D : (kind + 1) * D]
-
-    def k_copy(kind, n, d):
+        return kv.at[chunk * 8 + z, half, rows, :]
+
+    def k_copy(n, d):
         head = lax.rem(y + d, 4)
         return pltpu.make_async_remote_copy(
-            src_ref=cut((keys, values)[kind], head, D),
-            dst_ref=slot(kind, col, core, x_hi),
-            send_sem=k_send.at[kind, n, d],
-            recv_sem=k_recv.at[kind, col, x_hi],
+            src_ref=k_out.at[head],
+            dst_ref=slot(col, core, x_hi),
+            send_sem=k_send.at[n, d],
+            recv_sem=k_recv.at[col, x_hi],
             device_id=(z * 4 + n * 2 + lax.rem(y, 2), core * 4 + head),
             device_id_type=MESH,
         )
 
-    def k_local(kind):
+    def k_local():
         return pltpu.make_async_copy(
-            cut((keys, values)[kind], y, D),
-            slot(kind, col, core, x_hi),
-            k_recv.at[kind, col, x_hi],
+            k_out.at[y], slot(col, core, x_hi), k_recv.at[col, x_hi]
         )
 
     def k_each(act):
         for d in (1, 3, 2, 0):
+            if act:
+                for kind in range(2):
+                    k_stage(kind, d).wait()
             for n in range(2):
 
                 def one():
-                    for kind in range(2):
-                        copy = k_copy(kind, n, d)
-                        if act:
-                            copy.start()
-                        else:
-                            copy.wait_send()
+                    do(act, k_copy(n, d))
 
                 if d == 0:
                     pl.when(jnp.logical_not(selfish & (n == x_hi)))(one)
                 else:
                     one()
 
-    own_q = pltpu.make_async_copy(cut(queries, y, G * D), q_in.at[y], l_sem.at[0])
+    def do(act, copy):
+        if act:
+            copy.start()
+        else:
+            copy.wait_send()
+
+    def k_stage(kind, d):
+        head = lax.rem(y + d, 4)
+        return pltpu.make_async_copy(
+            cut((keys, values)[kind], head, D),
+            k_out.at[head, :, kind * D : (kind + 1) * D],
+            s_sem.at[kind, d],
+        )
+
+    def q_stage(d):
+        head = lax.rem(y + d, 4)
+        dst = q_in.at[y] if d == 0 else q_out.at[d - 1]
+        return pltpu.make_async_copy(cut(queries, head, G * D), dst, s_sem.at[2, d])
 
     def q_copy(d):
         return pltpu.make_async_remote_copy(
-            src_ref=cut(queries, lax.rem(y + d, 4), G * D),
+            src_ref=q_out.at[d - 1],
             dst_ref=q_in.at[y],
             send_sem=q_send.at[d - 1],
             recv_sem=q_recv.at[d - 1],
@@ -152,12 +168,11 @@
             device_id_type=MESH,
         ).wait_recv()
 
-    own_q.start()
-
-    @pl.when(selfish)
-    def _():
+    for d in (1, 3, 2, 0):
         for kind in range(2):
-            k_local(kind).start()
+            k_stage(kind, d).start()
+    for d in (1, 3, 2, 0):
+        q_stage(d).start()
 
     acc[...] = jnp.zeros_like(acc)
     top[...] = jnp.full_like(top, FLOOR)
@@ -181,7 +196,13 @@
 
     pl.semaphore_wait(barrier, 16 - jnp.where(selfish, 1, 0))
     k_each(True)
+
+    @pl.when(selfish)
+    def _():
+        k_local().start()
+
     for d in (1, 3, 2):
+        q_stage(d).wait()
         q_copy(d).start()
 
     def build(b):
@@ -263,12 +284,6 @@
             device_id_type=MESH,
         )
 
-    def do(act, copy):
-        if act:
-            copy.start()
-        else:
-            copy.wait_send()
-
     def spread_x(act, chunk, src):
         do(act, x_copy(chunk * 8 + src, lax.rem(chunk // 2 + src, 2)))
 
@@ -282,13 +297,14 @@
         for chunk, (_, _, on_up, on_down, wanted) in mine:
             if act:
                 for who in range(2):
-                    for kind in range(2):
-                        pltpu.make_async_copy(
-                            slot(kind, chunk, x_lo, who),
-                            slot(kind, chunk, x_lo, who),
-                            k_recv.at[kind, chunk, who],
-                        ).wait()
+                    pltpu.make_async_copy(
+                        k_out.at[0], slot(chunk, x_lo, who), k_recv.at[chunk, who]
+                    ).wait()
             piece = chunk * 8 + z
+
+            @pl.when(wanted)
+            def _():
+                spread_x(act, chunk, z)
 
             @pl.when(on_up)
             def _():
@@ -298,12 +314,8 @@
             def _():
                 do(act, c_copy(1, piece))
 
-            @pl.when(wanted)
-            def _():
-                spread_x(act, chunk, z)
-
-    def chain(t, act):
-        for chunk, (got_up, got_down, on_up, on_down, wanted) in mine:
+    def chain(t, act, part=slice(0, 4)):
+        for chunk, (got_up, got_down, on_up, on_down, wanted) in mine[part]:
             for way, (there, src) in enumerate(sides(t, got_up, got_down)):
 
                 @pl.when(there)
@@ -320,8 +332,8 @@
                     def _():
                         spread_x(act, chunk, src)
 
-    def across(t, act):
-        for chunk, (got_up, got_down, _, _, wanted) in mine:
+    def across(t, act, part=slice(0, 4)):
+        for chunk, (got_up, got_down, _, _, wanted) in mine[part]:
             for there, src in sides(t, got_up, got_down):
 
                 @pl.when(there & wanted)
@@ -424,13 +436,18 @@
         top[0:1, cols] = new
 
     chain_first(True)
-    own_q.wait()
+    q_stage(0).wait()
     build(y)
+    chain(1, True)
+    across_first(True)
+
+    def build_next(d, carry):
+        build(lax.rem(y + d, 4))
+        return carry
+
     for d in (1, 3, 2):
         q_wait(d)
-        build(lax.rem(y + 4 - d, 4))
-    chain(1, True)
-    across_first(True)
+    lax.fori_loop(1, 4, build_next, 0)
     from_twin_first()
     start = pieces(jnp.int32(0))
     ready(0, start)
@@ -439,12 +456,14 @@
     def step(i, carry):
         half = lax.rem(i, 2)
         now = pieces(i)
+        chain(i + 2, True, slice(0, 2))
+        across(i + 1, True, slice(0, 2))
         score(half, now, turn[1], 1)
         mix(half, 4, turn[0], 0)
+        chain(i + 2, True, slice(2, 4))
+        across(i + 1, True, slice(2, 4))
         score(half, now, turn[2], 0)
         mix(half, 4, turn[1], 1)
-        chain(i + 2, True)
-        across(i + 1, True)
         score(half, now, turn[3], 1)
         mix(half, 4, turn[2], 0)
         from_twin(i + 1)
@@ -471,7 +490,7 @@
             device_id_type=MESH,
         )
 
-    own_out = pltpu.make_async_copy(o_send.at[y], cut(out, y, G * D), l_sem.at[1])
+    own_out = pltpu.make_async_copy(o_send.at[y], cut(out, y, G * D), l_sem.at[0])
     for j in range(4):
         score(1, end, turn[j], 1)
         mix(0, 4, turn[j], 0)
@@ -525,6 +544,8 @@
         out_specs=anywhere,
         scratch_shapes=[
             pltpu.VMEM((4, 64, G * D), BF),
+            pltpu.VMEM((3, 64, G * D), BF),
+            pltpu.VMEM((4, 64, 2 * D), BF),
             pltpu.VMEM((64, 2, PIECE // 2, 2 * D), BF),
             pltpu.VMEM((4 * ROWS, 2 * D), BF),
             pltpu.VMEM((2, 5 * PIECE, D), BF),
@@ -534,8 +555,8 @@
             pltpu.VMEM((2, 5 * PIECE, ROWS), F32),
             pltpu.VMEM((2, 8, ROWS), F32),
             pltpu.VMEM((4, 64, G * D), BF),
-            dma((2, 2, 4)),
-            dma((2, 8, 2)),
+            dma((2, 4)),
+            dma((8, 2)),
             dma((3,)),
             dma((3,)),
             dma((3, 64)),
@@ -545,7 +566,8 @@
             dma((64,)),
             dma((3,)),
             dma((3,)),
-            dma((2,)),
+            dma((1,)),
+            dma((3, 4)),
         ],
         compiler_params=pltpu.CompilerParams(
             collective_id=0, has_side_effects=True, vmem_limit_bytes=60 * 2**20

time: 65.4 us -> 63.5 us (0.971)
  Pallas kernels: 63.2 us -> 61.5 us
    pallas_call x1, Pallas kernels: 63.2 us -> 61.5 us  [body(): pl.pallas_call(kernel, out_shape=jax.ShapeDtypeStruct(queries.shape, BF),...]
where the time goes in v4:
time: 63.5 us; the launch traced here: 63.4 us
  Pallas kernels  61.5 us (97%)
  local copies, waits for them, and re-layouts  1.87 us (3%)
    pallas_call x1, Pallas kernels, body(): pl.pallas_call(kernel, out_shape=jax.ShapeDtypeStruct(queries.shape, BF),...  61.5 us
    unnamed x1, local copies, waits for them, and re-layouts  1.87 us

profile of v4, /device:TPU:8, one launch (start us, length us, event | category | flops | bytes accessed | tf_op | source)
XLA Modules:
  0.0 63.4 jit_solution(14800911517842111235)
XLA Ops:
  0.0 61.5 %shard_map.46 = bf16[64,4096]{1,0:T(8,128)(2,1)} custom-call(s32[16]{0:T(128)} %lengths.1, bf16[64,4096]{1,0:T(8,128)(2,1)} %queries.1, bf16[64,512]{1,0:T(8,128)(2,1)} %keys.1, bf16[64,512]{1,0:T(8,128)(2,1)} %values.1), custom_call_target="tpu_custom_call" | custom-call | flops 12000000000 | bytes 10000000 | tf_op jit(solution)/shard_map/pallas_call | solution.py:540
  61.5 1.9 %copy.6 = bf16[64,4096]{1,0:T(8,128)(2,1)} copy(bf16[64,4096]{1,0:T(8,128)(2,1)} %shard_map.46) | data formatting | bytes 1048576

commit v5 on v4

--- a/solution.py
+++ b/solution.py
@@ -534,6 +534,10 @@
 
 
 def body(queries, keys, values, doc_lengths):
+    doc_lengths, queries, keys, values = (
+        pltpu.with_memory_space_constraint(a, pltpu.HBM)
+        for a in (doc_lengths, queries, keys, values)
+    )
     anywhere = pl.BlockSpec(memory_space=pl.ANY)
     hbm = pl.BlockSpec(memory_space=pltpu.HBM)
     dma = pltpu.SemaphoreType.DMA
@@ -570,7 +574,7 @@
             dma((3, 4)),
         ],
         compiler_params=pltpu.CompilerParams(
-            collective_id=0, has_side_effects=True, vmem_limit_bytes=60 * 2**20
+            collective_id=0, has_side_effects=True, vmem_limit_bytes=40 * 2**20
         ),
         cost_estimate=pl.CostEstimate(
             flops=12 * 10**9, bytes_accessed=10**7, transcendentals=18 * 10**6

time: 63.5 us -> 62.3 us (0.981)
  local copies, waits for them, and re-layouts: 1.87 us -> 0.8 us
    unnamed x1, local copies, waits for them, and re-layouts: 1.87 us -> 0.8 us
where the time goes in v5:
time: 62.3 us; the launch traced here: 62.2 us
  Pallas kernels  61.4 us (99%)
  local copies, waits for them, and re-layouts  0.8 us (1%)
    pallas_call x1, Pallas kernels, body(): pl.pallas_call(kernel, out_shape=jax.ShapeDtypeStruct(queries.shape, BF),...  61.4 us

profile of v5, /device:TPU:8, one launch (start us, length us, event | category | flops | bytes accessed | tf_op | source)
XLA Modules:
  0.0 62.2 jit_solution(4297857832623363110)
XLA Ops:
  0.0 61.4 %shard_map.46 = bf16[64,4096]{1,0:T(8,128)(2,1)S(1)} custom-call(s32[16]{0:T(128)} %lengths.1, bf16[64,4096]{1,0:T(8,128)(2,1)} %queries.1, bf16[64,512]{1,0:T(8,128)(2,1)} %keys.1, bf16[64,512]{1,0:T(8,128)(2,1)} %values.1), custom_call_target="tpu_custom_call" | custom-call | flops 12000000000 | bytes 10000000 | tf_op jit(solution)/shard_map/pallas_call | solution.py:544
  61.4 0.8 %copy.6 = bf16[64,4096]{1,0:T(8,128)(2,1)} copy(bf16[64,4096]{1,0:T(8,128)(2,1)S(1)} %shard_map.46) | data formatting | bytes 1048576

commit v6 on v5

--- a/solution.py
+++ b/solution.py
@@ -398,7 +398,8 @@
             seen = in_doc(spread(lax.broadcasted_iota(jnp.int32, (PIECE, D), 0)), chunk * 2048 + src * 256)
             lanes = lax.broadcasted_iota(jnp.int32, (PIECE, D), 1)
             flag = jnp.where(live, jnp.where(seen, 1.0, 0.0), jnp.where(lanes == 16, 1.0, 0.0))
-            kd[half, at, :] = flag.astype(BF)
+            kd[half, at, 0:D] = kv[piece, :, :, 0:D].reshape(PIECE, D)
+            kd[half, at, D : 2 * D] = flag.astype(BF)
 
     turn = [lax.rem(y + 1 + j, 4) for j in range(4)]
 
@@ -407,32 +408,32 @@
 
     def score(half, got, r, slot):
         q = q_aug[block(r), :]
-        best = None
-        for n, (chunk, src, *_) in enumerate(got):
-            at = slice(n * PIECE, (n + 1) * PIECE)
-            k = kv[chunk * 8 + src, :, :, 0:D].reshape(PIECE, D)
-            k = jnp.concatenate([k, kd[half, at, :]], axis=1)
-            s = lax.dot_general(k, q, (((1,), (1,)), ((), ())), preferred_element_type=F32)
-            if n == 4:
-                key = spread(lax.broadcasted_iota(jnp.int32, (PIECE, ROWS), 0))
-                query = r * 64 + (lax.broadcasted_iota(jnp.int32, (PIECE, ROWS), 1) & 63)
-                s = jnp.where(key <= query, s, HIDE)
+        wide = 4 * PIECE
+        s = lax.dot_general(
+            kd[half, 0:wide, :], q, (((1,), (1,)), ((), ())), preferred_element_type=F32
+        )
+        sb[slot, 0:wide, :] = s
+        best = jnp.max(s, axis=0, keepdims=True)
+        if len(got) == 5:
+            at = slice(wide, wide + PIECE)
+            s = lax.dot_general(
+                kd[half, at, :], q, (((1,), (1,)), ((), ())), preferred_element_type=F32
+            )
+            key = spread(lax.broadcasted_iota(jnp.int32, (PIECE, ROWS), 0))
+            query = r * 64 + (lax.broadcasted_iota(jnp.int32, (PIECE, ROWS), 1) & 63)
+            s = jnp.where(key <= query, s, HIDE)
             sb[slot, at, :] = s
-            here = jnp.max(s, axis=0, keepdims=True)
-            best = here if best is None else jnp.maximum(best, here)
+            best = jnp.maximum(best, jnp.max(s, axis=0, keepdims=True))
         mb[slot, 0:1, :] = best
 
     def mix(half, count, r, slot):
         cols = block(r)
         old = top[0:1, cols]
         new = jnp.maximum(old, mb[slot, 0:1, :])
-        shift = new * SCALE
+        at = slice(0, count * PIECE)
+        w = jnp.exp2(sb[slot, at, :] * SCALE - new * SCALE).astype(BF)
         sums = acc[:, cols] * jnp.exp2((old - new) * SCALE)
-        for n in range(count):
-            at = slice(n * PIECE, (n + 1) * PIECE)
-            w = jnp.exp2(sb[slot, at, :] * SCALE - shift).astype(BF)
-            sums = sums + jnp.dot(vt[half, :, at], w, preferred_element_type=F32)
-        acc[:, cols] = sums
+        acc[:, cols] = sums + jnp.dot(vt[half, :, at], w, preferred_element_type=F32)
         top[0:1, cols] = new
 
     chain_first(True)
@@ -552,7 +553,7 @@
             pltpu.VMEM((4, 64, 2 * D), BF),
             pltpu.VMEM((64, 2, PIECE // 2, 2 * D), BF),
             pltpu.VMEM((4 * ROWS, 2 * D), BF),
-            pltpu.VMEM((2, 5 * PIECE, D), BF),
+            pltpu.VMEM((2, 5 * PIECE, 2 * D), BF),
             pltpu.VMEM((2, VR, 5 * PIECE), BF),
             pltpu.VMEM((VR, 4 * ROWS), F32),
             pltpu.VMEM((8, 4 * ROWS), F32),

time: 62.3 us -> 61.8 us (level)
  no operation moved by 1% of the time
where the time goes in v6:
time: 61.8 us; the launch traced here: 61.7 us
  Pallas kernels  60.9 us (99%)
  local copies, waits for them, and re-layouts  0.8 us (1%)
    pallas_call x1, Pallas kernels, body(): pl.pallas_call(kernel, out_shape=jax.ShapeDtypeStruct(queries.shape, BF),...  60.9 us

profile of v6, /device:TPU:8, one launch (start us, length us, event | category | flops | bytes accessed | tf_op | source)
XLA Modules:
  0.0 61.7 jit_solution(11391776941356975105)
XLA Ops:
  0.0 60.9 %shard_map.46 = bf16[64,4096]{1,0:T(8,128)(2,1)S(1)} custom-call(s32[16]{0:T(128)} %lengths.1, bf16[64,4096]{1,0:T(8,128)(2,1)} %queries.1, bf16[64,512]{1,0:T(8,128)(2,1)} %keys.1, bf16[64,512]{1,0:T(8,128)(2,1)} %values.1), custom_call_target="tpu_custom_call" | custom-call | flops 12000000000 | bytes 10000000 | tf_op jit(solution)/shard_map/pallas_call | solution.py:545
  60.9 0.8 %copy.6 = bf16[64,4096]{1,0:T(8,128)(2,1)} copy(bf16[64,4096]{1,0:T(8,128)(2,1)S(1)} %shard_map.46) | data formatting | bytes 1048576
